TPU v7x, 128 devices: a whole 4x4x4 slice. The times are simulated.
128 devices in a mesh: grp: 8 (over x, core), sub: 16 (over y, z).
Axes of the slice: x: 4, y: 4, z: 4, core: 2. Of those that a mesh axis runs over, the one named last changes fastest.
Arguments:
- currents: bfloat16 [128, 1048576], P(None, ('grp', 'sub')), may hold values from -6 to 6
- leaf_segment_count: int32 [128, 64], P(('grp', 'sub')), may hold values from 1 to 128, 6144 in all within a row
- leaf_basis: bfloat16 [8192, 128, 64], P(('grp', 'sub')), may hold values from -0.5 to 0.5
- transfers: bfloat16 [16128, 64, 64], P(('grp', 'sub')), may hold values from -0.625 to 0.625
- coupling: bfloat16 [16256, 6, 64, 64], P(('grp', 'sub')), may hold values from -0.3125 to 0.3125
- far_sources: int32 [16256, 6], P(('grp', 'sub')), may hold values from 0 to 8191, as said below
- near_tiles: bfloat16 [8192, 5, 128, 128], P(('grp', 'sub')), may hold values from -0.25 to 0.25
- near_sources: int32 [8192, 5], P(('grp', 'sub')), may hold values from 0 to 8191, as said below
Outputs:
- voltages: float32 [128, 1048576], P(None, ('grp', 'sub'))
Inputs may be any that keep to these rules, and one draw needn't show every extreme that they name: `far_sources`: the sources of a target at levels 0 and 1 lie in its group and differ from it by at most 8 in cluster index; at levels 2 to 5 they lie in its group; at level 6 they are any of the 128 clusters. `near_sources`: Near-field sources of a leaf lie in its group and differ from it by at most 2 in leaf index; slot 0 is the leaf itself.
All inputs are finite; a program needn't handle non-finite values.
Results may differ from a plain program's by a relative error of at most 0.024.
Values may be sent and summed in bfloat16 or wider, within the bound.
A program may use at most 192 MiB of HBM per device.

v0:
```python
import functools

import jax
import jax.numpy as jnp
from jax import lax
from jax.experimental import pallas as pl
from jax.experimental.pallas import tpu as pltpu
from jax.sharding import PartitionSpec as P

LEVELS = 6
REACH = 8
NEAR_REACH = 2
SIDE = 4
SUBS = 16
XS = 4
F32 = jnp.float32
BF16 = jnp.bfloat16
VMEM_LIMIT = 60 * 1024 * 1024

C_STRIDE = 72
C_ROWS = 127 * C_STRIDE
E_STRIDE = 40
NT = (((1,), (1,)), ((), ()))
TN = (((0,), (0,)), ((), ()))


def span(level):
    count = 64 >> level
    return 128 - 2 * count, count


STEPS = (
    (None, 0, 0, 0, 0, 1),
    (None, 0, 0, 0, 0, -1),
    (None, 0, 0, 0, 1, 1),
    (None, 0, 0, 0, 1, -1),
    (0, -1, 0, 1, 0, 1),
    (0, -1, 0, 0, 1, 1),
    (0, -1, 0, 0, 1, -1),
    (1, 1, 0, 2, 0, -1),
    (1, 1, 0, 0, 1, 1),
    (1, 1, 0, 0, 1, -1),
    (2, 0, -1, 1, 1, 1),
    (3, 0, 1, 2, 1, -1),
    (4, 2, 0, 1, 1, 1),
    (4, 2, 0, 1, 1, -1),
    (7, 2, 0, 2, 1, 1),
    (7, 2, 0, 2, 1, -1),
    (8, 1, -1, 0, 1, 1),
    (6, -1, 1, 0, 1, -1),
    (12, 2, -1, 1, 1, 1),
    (15, 2, 1, 2, 1, -1),
)
N_STEPS = len(STEPS)
WAVES = ((0, 1, 2, 3), (4, 7, 8, 6), (12, 15), (5, 9, 10, 11, 13, 14, 16, 17, 18, 19))

TREES = (
    ("g2", 16, 0, 8, True),
    ("g2", 16, 8, 8, False),
    ("g35", 14, 0, 8, True),
    ("g35", 14, 8, 6, False),
)
CHUNKS = 8


def main_kernel(
    cnt, currents, basis, transfers, coupling, near_tiles, far, near,
    partial_out, joined_out, d1_out,
    cur, bas, tr, e32, xm, x0, x1, g2, g35, roots, cin, c32, tiles, fields, partial, joined, d,
    in_sem, out_sem, halo_send, halo_recv, tree_send, tree_recv,
    root_send, root_recv, xs_send, xs_recv, core_send, core_recv,
):
    grp = lax.axis_index("grp")
    sub = lax.axis_index("sub")
    y = sub // SIDE
    z = sub % SIDE
    core = grp % 2
    x = grp // 2
    mine = grp * SUBS + sub

    def at(dy, dz):
        return ((y + dy + SIDE) % SIDE) * SIDE + (z + dz + SIDE) % SIDE

    def along_x(i):
        return ((x + i) % XS) * 2 + core

    other_core = x * 2 + (1 - core)

    loads = [
        pltpu.make_async_copy(src, dst, in_sem.at[i])
        for i, (src, dst) in enumerate(
            ((transfers, tr), (currents, cur), (basis, bas), (coupling, cin), (near_tiles, tiles))
        )
    ]
    for copy in loads:
        copy.start()

    barrier = pltpu.get_barrier_semaphore()

    def greet(device):
        pl.semaphore_signal(
            barrier, inc=1, device_id=device, device_id_type=pl.DeviceIdType.MESH
        )

    for i in range(1, SUBS):
        greet((grp, (sub + i) % SUBS))
    for i in range(1, XS):
        greet((along_x(i), sub))
    greet((other_core, sub))

    def remote(src, dst, send, recv, device):
        return pltpu.make_async_remote_copy(
            src_ref=src, dst_ref=dst, send_sem=send, recv_sem=recv,
            device_id=device, device_id_type=pl.DeviceIdType.MESH,
        )

    up, down = (grp, (sub + 1) % SUBS), (grp, (sub + SUBS - 1) % SUBS)
    halos = []
    for i, (buffer, width, count) in enumerate(
        ((xm, NEAR_REACH, 64), (x0, REACH, 64), (x1, REACH, 32))
    ):
        halos.append(
            (
                remote(buffer.at[pl.ds(count, width)], buffer.at[pl.ds(0, width)],
                       halo_send.at[2 * i], halo_recv.at[2 * i], up),
                remote(buffer.at[pl.ds(width, width)], buffer.at[pl.ds(count + width, width)],
                       halo_send.at[2 * i + 1], halo_recv.at[2 * i + 1], down),
            )
        )

    def step_copy(tree, i):
        name, n, low, width, z_first = TREES[tree]
        buffer = g2 if name == "g2" else g35
        _, first, second, part, dim, way = STEPS[i]
        offset = (second, first) if z_first else (first, second)
        move = (way, 0) if (dim == 1) == z_first else (0, way)
        half = width // 2
        skip, rows = ((0, width), (0, half), (half, width - half))[part]
        block = buffer.at[pl.ds(at(*offset) * n + low + skip, rows)]
        return remote(block, block, tree_send.at[tree * N_STEPS + i],
                      tree_recv.at[tree * N_STEPS + i], (grp, at(*move)))

    copies = [[step_copy(tree, i) for i in range(N_STEPS)] for tree in range(len(TREES))]

    def begin(tree):
        for i in range(4):
            copies[tree][i].start()

    def wave(tree, k):
        for i in WAVES[k]:
            copies[tree][i].wait_recv()
            for j in range(N_STEPS):
                if STEPS[j][0] == i:
                    copies[tree][j].start()


    def relayout_e(k, carry):
        slab = jnp.concatenate([tr[k], tr[k + 32]], axis=0).astype(F32)
        e32[pl.ds(k, 126, stride=E_STRIDE), :] = slab.T
        return carry

    def transfer(t, count):
        parts = []
        for c in range(count):
            rows = e32[pl.ds(pl.multiple_of((t + c) * E_STRIDE, 8), 32), :].astype(BF16)
            parts += [rows[:, :64], rows[:, 64:]]
        return jnp.concatenate(parts, axis=0)

    loads[0].wait()
    lax.fori_loop(0, 32, relayout_e, 0, unroll=4)
    loads[1].wait()
    loads[2].wait()

    lane = lax.broadcasted_iota(jnp.int32, (1, 128), 1)

    def leaf(l, carry):
        live = (lane < cnt[0, l]).astype(F32).astype(BF16)
        m = cur[:, pl.ds(pl.multiple_of(l * 128, 128), 128)] * live
        xm[NEAR_REACH + l] = m
        c = lax.dot_general(bas[l], m, NT, preferred_element_type=F32)
        x0[REACH + l] = c.astype(BF16)
        return carry

    def lift(level, src, src_at, dst, dst_at, low, count, unroll):
        start, _ = span(level - 1)

        def parent(i, carry):
            p = low + i
            pair = src[pl.ds(src_at + 2 * p, 2)].reshape(128, 128)
            c = lax.dot_general(transfer(start + 2 * p, 2), pair, TN, preferred_element_type=F32)
            dst[dst_at + p] = c.astype(BF16)
            return carry

        lax.fori_loop(0, count, parent, 0, unroll=unroll)

    slot2, slot35 = sub * 16, sub * 14
    for h in range(2):
        lax.fori_loop(32 * h, 32 * (h + 1), leaf, 0, unroll=8)
        if h == 0:
            pl.semaphore_wait(barrier, SUBS - 1 + XS - 1 + 1)
        halos[0][1 - h].start()
        halos[1][1 - h].start()
        lift(1, x0, REACH, x1, REACH, 16 * h, 16, 8)
        halos[2][1 - h].start()
        lift(2, x1, REACH, g2, slot2, 8 * h, 8, 8)
        begin(h)
    lift(3, g2, slot2, g35, slot35, 0, 8, 8)
    begin(2)
    lift(4, g35, slot35, g35, slot35 + 8, 0, 4, 4)
    lift(5, g35, slot35 + 8, g35, slot35 + 12, 0, 2, 2)
    begin(3)
    lift(6, g35, slot35 + 12, roots, mine, 0, 1, 1)
    root_row = roots.at[pl.ds(mine, 1)]
    root_copies = [
        remote(root_row, root_row, root_send.at[i - 1], root_recv.at[i - 1],
               (grp, (sub + i) % SUBS))
        for i in range(1, SUBS)
    ]
    for copy in root_copies:
        copy.start()


    def relayout_c(low, high):
        def one(a, carry):
            for qp in range(3):
                slab = cin[pl.ds(2 * qp, 2), a].reshape(128, 127).astype(F32)
                c32[pl.ds(qp * C_ROWS + a, 127, stride=C_STRIDE), :] = slab.T
            return carry

        lax.fori_loop(low, high, one, 0, unroll=2)

    def couple(level, buffer, place, low, count, unroll):
        start, _ = span(level)
        last = buffer.shape[0] - 1

        def target(i, carry):
            t = start + low + i
            matrix = jnp.concatenate(
                [
                    c32[pl.ds(pl.multiple_of(qp * C_ROWS + t * C_STRIDE, 8), 64), :].astype(BF16)
                    for qp in range(3)
                ],
                axis=1,
            )
            stacked = jnp.concatenate(
                [buffer[jnp.clip(place(far[q, t]), 0, last)] for q in range(6)], axis=0
            )
            fields[t] = jnp.dot(matrix, stacked, preferred_element_type=F32)
            return carry

        lax.fori_loop(0, count, target, 0, unroll=unroll)

    def join(low, count):
        def one(i, carry):
            l = low + i
            got = lax.dot_general(transfer(l, 1), bas[l], TN, preferred_element_type=F32)
            joined[l] = got.astype(BF16)
            return carry

        lax.fori_loop(0, count, one, 0, unroll=4)

    near_base = mine * 64 - NEAR_REACH
    outs = []

    def near_field(low, count):
        def one(i, carry):
            t = low + i
            total = lax.dot_general(
                fields[t].astype(BF16), bas[t], TN, preferred_element_type=F32
            )
            rows = jnp.concatenate(
                [
                    xm[jnp.clip(near[q, t] - near_base, 0, 64 + 2 * NEAR_REACH - 1)]
                    for q in range(5)
                ],
                axis=1,
            )
            blocks = jnp.concatenate([tiles[t, q] for q in range(5)], axis=1)
            total = total + lax.dot_general(rows, blocks, NT, preferred_element_type=F32)
            partial[t] = total.astype(BF16)
            return carry

        lax.fori_loop(0, count, one, 0, unroll=4)
        block = pl.ds(low, count)
        copy = pltpu.make_async_copy(
            partial.at[block], partial_out.at[block], out_sem.at[1 + low // count]
        )
        copy.start()
        outs.append(copy)

    place0 = lambda s: s - (mine * 64 - REACH)
    place1 = lambda s: s - (mine * 32 - REACH)

    loads[3].wait()
    relayout_c(0, 16)
    wave(0, 0)
    relayout_c(16, 32)
    wave(1, 0)
    relayout_c(32, 48)
    wave(2, 0)
    relayout_c(48, 64)
    wave(3, 0)

    for copy in root_copies:
        copy.wait_recv()
    block = roots.at[pl.ds(grp * SUBS, SUBS)]
    x_copies = [
        remote(block, block, xs_send.at[i - 1], xs_recv.at[i - 1], (along_x(i), sub))
        for i in range(1, XS)
    ]
    for copy in x_copies:
        copy.start()
    core_copies = []
    for i in range(XS):
        held = roots.at[pl.ds(along_x(i) * SUBS, SUBS)]
        core_copies.append(
            remote(held, held, core_send.at[i], core_recv.at[i], (other_core, sub))
        )
    core_copies[0].start()

    for i in range(2):
        halos[1][i].wait_recv()
    couple(0, x0, place0, 0, 32, 8)
    wave(0, 1)
    couple(0, x0, place0, 32, 32, 8)
    wave(1, 1)
    join(0, 64)
    copy = pltpu.make_async_copy(joined, joined_out, out_sem.at[0])
    copy.start()
    outs.append(copy)
    wave(2, 1)
    loads[4].wait()
    for i in range(2):
        halos[0][i].wait_recv()
    width = 64 // CHUNKS
    near_field(0, width)
    near_field(width, width)
    wave(3, 1)
    near_field(2 * width, width)
    near_field(3 * width, width)
    wave(0, 2)
    near_field(4 * width, width)
    near_field(5 * width, width)
    wave(1, 2)
    near_field(6 * width, width)
    near_field(7 * width, width)
    wave(2, 2)
    for copy in x_copies:
        copy.wait_recv()
    for copy in core_copies[1:]:
        copy.start()
    for i in range(2):
        halos[2][i].wait_recv()
    couple(1, x1, place1, 0, 32, 8)
    wave(3, 2)
    for copy in core_copies:
        copy.wait_recv()
    couple(6, roots, lambda s: s, 0, 1, 1)

    def place35(level, offset):
        _, count = span(level)

        def place(s):
            relative = s - grp * SUBS * count
            return (relative // count) * 14 + offset + relative % count

        return place

    wave(2, 3)
    wave(3, 3)
    couple(3, g35, place35(3, 0), 0, 8, 8)
    couple(4, g35, place35(4, 8), 0, 4, 4)
    couple(5, g35, place35(5, 12), 0, 2, 2)
    wave(0, 3)
    wave(1, 3)
    couple(2, g2, lambda s: s - grp * SUBS * 16, 0, 16, 8)


    d[126] = fields[126].astype(BF16)
    for level in range(LEVELS - 1, 0, -1):
        start, _ = span(level)
        parents, count = span(level + 1)

        def parent(p, carry, start=start, parents=parents, level=level):
            got = jnp.dot(
                transfer(start + 2 * p, 2), d[parents + p], preferred_element_type=F32
            )
            got = got + fields[pl.ds(start + 2 * p, 2)].reshape(128, 128)
            got = got.reshape(2, 64, 128).astype(BF16)
            if level == 1:
                d1_out[pl.ds(2 * p, 2)] = got
            else:
                d[pl.ds(start + 2 * p, 2)] = got
            return carry

        lax.fori_loop(0, count, parent, 0, unroll=min(count, 8))

    for copy in root_copies + [c for pair in halos for c in pair] + x_copies + core_copies:
        copy.wait_send()
    for tree in copies:
        for copy in tree:
            copy.wait_send()
    for copy in outs:
        copy.wait()


def main_pass(cnt, currents, basis, tr, matrices, near_tiles, far, near):
    vm = pl.BlockSpec(memory_space=pltpu.VMEM)
    hbm = pl.BlockSpec(memory_space=pl.ANY)
    sm = pl.BlockSpec(memory_space=pltpu.SMEM)
    dma = pltpu.SemaphoreType.DMA
    steps = len(TREES) * N_STEPS
    return pl.pallas_call(
        main_kernel,
        out_shape=(
            jax.ShapeDtypeStruct((64, 128, 128), BF16),
            jax.ShapeDtypeStruct((64, 64, 128), BF16),
            jax.ShapeDtypeStruct((32, 64, 128), BF16),
        ),
        in_specs=[sm, hbm, hbm, hbm, hbm, hbm, sm, sm],
        out_specs=(hbm, hbm, vm),
        scratch_shapes=[
            pltpu.VMEM((128, 8192), BF16),
            pltpu.VMEM((64, 64, 128), BF16),
            pltpu.VMEM((64, 64, 126), BF16),
            pltpu.VMEM((126 * E_STRIDE, 128), F32),
            pltpu.VMEM((64 + 2 * NEAR_REACH, 128, 128), BF16),
            pltpu.VMEM((64 + 2 * REACH, 64, 128), BF16),
            pltpu.VMEM((32 + 2 * REACH, 64, 128), BF16),
            pltpu.VMEM((256, 64, 128), BF16),
            pltpu.VMEM((224, 64, 128), BF16),
            pltpu.VMEM((128, 64, 128), BF16),
            pltpu.VMEM((6, 64, 64, 127), BF16),
            pltpu.VMEM((3 * C_ROWS, 128), F32),
            pltpu.VMEM((64, 5, 128, 128), BF16),
            pltpu.VMEM((127, 64, 128), F32),
            pltpu.VMEM((64, 128, 128), BF16),
            pltpu.VMEM((64, 64, 128), BF16),
            pltpu.VMEM((127, 64, 128), BF16),
            dma((5,)), dma((1 + CHUNKS,)),
            dma((6,)), dma((6,)),
            dma((steps,)), dma((steps,)),
            dma((SUBS - 1,)), dma((SUBS - 1,)),
            dma((XS - 1,)), dma((XS - 1,)),
            dma((XS,)), dma((XS,)),
        ],
        compiler_params=pltpu.CompilerParams(
            collective_id=0, has_side_effects=True, vmem_limit_bytes=VMEM_LIMIT
        ),
        name="main_pass",
    )(cnt, currents, basis, tr, matrices, near_tiles, far, near)


BLOCK = 8


def last_kernel(cnt, d1, joined, partial, out):
    g = pl.program_id(0)
    lane = lax.broadcasted_iota(jnp.int32, (1, 128), 1)
    for i in range(BLOCK):
        smooth = lax.dot_general(d1[i // 2], joined[i], TN, preferred_element_type=F32)
        live = (lane < cnt[0, g * BLOCK + i]).astype(F32)
        out[:, i * 128 : (i + 1) * 128] = (smooth + partial[i].astype(F32)) * live


def last_pass(cnt, d1, joined, partial):
    return pl.pallas_call(
        last_kernel,
        grid=(64 // BLOCK,),
        out_shape=jax.ShapeDtypeStruct((128, 8192), F32),
        in_specs=[
            pl.BlockSpec(memory_space=pltpu.SMEM),
            pl.BlockSpec((BLOCK // 2, 64, 128), lambda g: (g, 0, 0)),
            pl.BlockSpec((BLOCK, 64, 128), lambda g: (g, 0, 0)),
            pl.BlockSpec((BLOCK, 128, 128), lambda g: (g, 0, 0)),
        ],
        out_specs=pl.BlockSpec((128, BLOCK * 128), lambda g: (0, g)),
        compiler_params=pltpu.CompilerParams(vmem_limit_bytes=VMEM_LIMIT),
        name="last_pass",
    )(cnt, d1, joined, partial)


def body(
    currents,
    leaf_segment_count,
    leaf_basis,
    transfers,
    coupling,
    far_sources,
    near_tiles,
    near_sources,
):
    basis = jnp.transpose(leaf_basis, (0, 2, 1))
    tr = jnp.transpose(transfers, (1, 2, 0))
    matrices = jnp.transpose(coupling, (1, 2, 3, 0))
    far = jnp.transpose(far_sources, (1, 0))
    near = jnp.transpose(near_sources, (1, 0))
    partial, joined, d1 = main_pass(
        leaf_segment_count, currents, basis, tr, matrices, near_tiles, far, near
    )
    return last_pass(leaf_segment_count, d1, joined, partial)


def solution(mesh):
    return jax.shard_map(
        body,
        mesh=mesh,
        in_specs=(
            P(None, ("grp", "sub")),
            P(("grp", "sub"), None),
            P(("grp", "sub"), None, None),
            P(("grp", "sub"), None, None),
            P(("grp", "sub"), None, None, None),
            P(("grp", "sub"), None),
            P(("grp", "sub"), None, None, None),
            P(("grp", "sub"), None),
        ),
        out_specs=P(None, ("grp", "sub")),
        check_vma=False,
    )
```

profile of v0, /device:TPU:0, one launch (start us, length us, event | category | flops | bytes accessed | tf_op | source)
XLA Modules:
  0.0 74.3 jit_solution(3705473333388481474)
XLA Ops:
  0.0 66.8 %main_pass.1 = (bf16[64,128,128]{2,1,0:T(8,128)(2,1)}, bf16[64,64,128]{2,1,0:T(8,128)(2,1)}, bf16[32,64,128]{2,1,0:T(8,128)(2,1)}) custom-call(s32[1,64]{1,0:T(1,128)} %cnt.3, bf16[128,8192]{1,0:T(8,128)(2,1)} %currents.1, bf16[64,64,128]{2,1,0:T(8,128)(2,1)} %bitcast.6, bf16[64,64,126]{2,1,0:T(8,128)(2,1)} %bitcast.7, bf16[6,64,64,127]{3,2,1,0:T(8,128)(2,1)} %bitcast.5, ...), custom_call_target="tpu_custom_call" | custom-call | tf_op jit(solution)/shard_map/main_pass/pallas_call | solution.py:413
  66.8 7.5 %last_pass.1 = f32[128,8192]{1,0:T(8,128)} custom-call(s32[1,64]{1,0:T(1,128)} %cnt.3, bf16[32,64,128]{2,1,0:T(8,128)(2,1)} %get-tuple-element.8.d1, bf16[64,64,128]{2,1,0:T(8,128)(2,1)} %get-tuple-element.9.joined, bf16[64,128,128]{2,1,0:T(8,128)(2,1)} %get-tuple-element.10.partial), custom_call_target="tpu_custom_call" | custom-call | tf_op jit(solution)/shard_map/last_pass/pallas_call | solution.py:467
where the time goes:
time: 74.5 us; the launch traced here: 74.3 us
  Pallas kernels  74.2 us (100%)
    pallas_call x1, Pallas kernels, main_pass(): pl.pallas_call(main_kernel, out_shape=(jax.ShapeDtypeStruct((64, 128, 128...  66.8 us
    pallas_call x1, Pallas kernels, last_pass(): pl.pallas_call(last_kernel, grid=(64 // BLOCK,), out_shape=jax.ShapeDtype...  7.46 us

commit v1 on v0

--- a/solution.py
+++ b/solution.py
@@ -20,6 +20,7 @@
 C_STRIDE = 72
 C_ROWS = 127 * C_STRIDE
 E_STRIDE = 40
+ROOT_ROWS = 4
 NT = (((1,), (1,)), ((), ()))
 TN = (((0,), (0,)), ((), ()))
 
@@ -59,16 +60,18 @@
     ("g2", 16, 8, 8, False),
     ("g35", 14, 0, 8, True),
     ("g35", 14, 8, 6, False),
+    ("roots", ROOT_ROWS, 0, ROOT_ROWS, True),
 )
+ROOT_TREE = 4
 CHUNKS = 8
 
 
 def main_kernel(
     cnt, currents, basis, transfers, coupling, near_tiles, far, near,
-    partial_out, joined_out, d1_out,
-    cur, bas, tr, e32, xm, x0, x1, g2, g35, roots, cin, c32, tiles, fields, partial, joined, d,
+    partial_out, joined_out, d2_out,
+    cur, bas, tr, e32, xm, x0, x1, g2, g35, roots, cin, c32, tiles, fields, partial, joined, joined2, d,
     in_sem, out_sem, halo_send, halo_recv, tree_send, tree_recv,
-    root_send, root_recv, xs_send, xs_recv, core_send, core_recv,
+    xs_send, xs_recv, core_send, core_recv,
 ):
     grp = lax.axis_index("grp")
     sub = lax.axis_index("sub")
@@ -130,13 +133,14 @@
 
     def step_copy(tree, i):
         name, n, low, width, z_first = TREES[tree]
-        buffer = g2 if name == "g2" else g35
+        buffer = {"g2": g2, "g35": g35, "roots": roots}[name]
         _, first, second, part, dim, way = STEPS[i]
         offset = (second, first) if z_first else (first, second)
         move = (way, 0) if (dim == 1) == z_first else (0, way)
         half = width // 2
         skip, rows = ((0, width), (0, half), (half, width - half))[part]
-        block = buffer.at[pl.ds(at(*offset) * n + low + skip, rows)]
+        slot = at(*offset) + (grp * SUBS if name == "roots" else 0)
+        block = buffer.at[pl.ds(slot * n + low + skip, rows)]
         return remote(block, block, tree_send.at[tree * N_STEPS + i],
                       tree_recv.at[tree * N_STEPS + i], (grp, at(*move)))
 
@@ -203,21 +207,19 @@
         lift(1, x0, REACH, x1, REACH, 16 * h, 16, 8)
         halos[2][1 - h].start()
         lift(2, x1, REACH, g2, slot2, 8 * h, 8, 8)
-        begin(h)
+        if h == 0:
+            begin(0)
     lift(3, g2, slot2, g35, slot35, 0, 8, 8)
-    begin(2)
     lift(4, g35, slot35, g35, slot35 + 8, 0, 4, 4)
     lift(5, g35, slot35 + 8, g35, slot35 + 12, 0, 2, 2)
+    start6, _ = span(LEVELS - 1)
+    pair = g35[pl.ds(slot35 + 12, 2)].reshape(128, 128)
+    root = lax.dot_general(transfer(start6, 2), pair, TN, preferred_element_type=F32)
+    roots[pl.ds(mine * ROOT_ROWS, ROOT_ROWS)] = root.astype(BF16).reshape(ROOT_ROWS, 16, 128)
+    begin(ROOT_TREE)
     begin(3)
-    lift(6, g35, slot35 + 12, roots, mine, 0, 1, 1)
-    root_row = roots.at[pl.ds(mine, 1)]
-    root_copies = [
-        remote(root_row, root_row, root_send.at[i - 1], root_recv.at[i - 1],
-               (grp, (sub + i) % SUBS))
-        for i in range(1, SUBS)
-    ]
-    for copy in root_copies:
-        copy.start()
+    begin(2)
+    begin(1)
 
 
     def relayout_c(low, high):
@@ -231,7 +233,12 @@
 
     def couple(level, buffer, place, low, count, unroll):
         start, _ = span(level)
-        last = buffer.shape[0] - 1
+        rows = ROOT_ROWS if level == LEVELS else 1
+        last = buffer.shape[0] // rows - 1
+
+        def source(q, t):
+            i = jnp.clip(place(far[q, t]), 0, last)
+            return buffer[i] if rows == 1 else buffer[pl.ds(i * rows, rows)].reshape(64, 128)
 
         def target(i, carry):
             t = start + low + i
@@ -242,19 +249,31 @@
                 ],
                 axis=1,
             )
-            stacked = jnp.concatenate(
-                [buffer[jnp.clip(place(far[q, t]), 0, last)] for q in range(6)], axis=0
-            )
-            fields[t] = jnp.dot(matrix, stacked, preferred_element_type=F32)
+            stacked = jnp.concatenate([source(q, t) for q in range(6)], axis=0)
+            got = jnp.dot(matrix, stacked, preferred_element_type=F32)
+            if level == 2:
+                d2_out[low + i] = (fields[t] + got).astype(BF16)
+            else:
+                fields[t] = got
             return carry
 
         lax.fori_loop(0, count, target, 0, unroll=unroll)
 
     def join(low, count):
         def one(i, carry):
-            l = low + i
-            got = lax.dot_general(transfer(l, 1), bas[l], TN, preferred_element_type=F32)
-            joined[l] = got.astype(BF16)
+            p = low + i
+            pair = []
+            for c in range(2):
+                l = 2 * p + c
+                got = lax.dot_general(transfer(l, 1), bas[l], TN, preferred_element_type=F32)
+                pair.append(got.astype(BF16))
+                joined[l] = pair[-1]
+            got = lax.dot_general(
+                transfer(64 + p, 1), jnp.concatenate(pair, axis=1), TN,
+                preferred_element_type=F32,
+            ).astype(BF16)
+            joined2[2 * p] = got[:, :128]
+            joined2[2 * p + 1] = got[:, 128:]
             return carry
 
         lax.fori_loop(0, count, one, 0, unroll=4)
@@ -265,8 +284,10 @@
     def near_field(low, count):
         def one(i, carry):
             t = low + i
+            both = jnp.concatenate([fields[t], fields[64 + t // 2]], axis=0).astype(BF16)
             total = lax.dot_general(
-                fields[t].astype(BF16), bas[t], TN, preferred_element_type=F32
+                both, jnp.concatenate([bas[t], joined[t]], axis=0), TN,
+                preferred_element_type=F32,
             )
             rows = jnp.concatenate(
                 [
@@ -294,28 +315,32 @@
     loads[3].wait()
     relayout_c(0, 16)
     wave(0, 0)
+    wave(ROOT_TREE, 0)
     relayout_c(16, 32)
-    wave(1, 0)
+    wave(3, 0)
+    wave(ROOT_TREE, 1)
     relayout_c(32, 48)
     wave(2, 0)
+    wave(ROOT_TREE, 2)
     relayout_c(48, 64)
-    wave(3, 0)
-
-    for copy in root_copies:
-        copy.wait_recv()
-    block = roots.at[pl.ds(grp * SUBS, SUBS)]
+    wave(1, 0)
+    wave(ROOT_TREE, 3)
+
+    def group_roots(g):
+        return roots.at[pl.ds(g * SUBS * ROOT_ROWS, SUBS * ROOT_ROWS)]
+
+    block = group_roots(grp)
     x_copies = [
         remote(block, block, xs_send.at[i - 1], xs_recv.at[i - 1], (along_x(i), sub))
         for i in range(1, XS)
     ]
     for copy in x_copies:
         copy.start()
-    core_copies = []
-    for i in range(XS):
-        held = roots.at[pl.ds(along_x(i) * SUBS, SUBS)]
-        core_copies.append(
-            remote(held, held, core_send.at[i], core_recv.at[i], (other_core, sub))
-        )
+    core_copies = [
+        remote(group_roots(along_x(i)), group_roots(along_x(i)), core_send.at[i],
+               core_recv.at[i], (other_core, sub))
+        for i in range(XS)
+    ]
     core_copies[0].start()
 
     for i in range(2):
@@ -323,36 +348,37 @@
     couple(0, x0, place0, 0, 32, 8)
     wave(0, 1)
     couple(0, x0, place0, 32, 32, 8)
+    wave(3, 1)
+    for i in range(2):
+        halos[2][i].wait_recv()
+    couple(1, x1, place1, 0, 32, 8)
+    wave(2, 1)
+    join(0, 16)
     wave(1, 1)
-    join(0, 64)
-    copy = pltpu.make_async_copy(joined, joined_out, out_sem.at[0])
+    join(16, 16)
+    copy = pltpu.make_async_copy(joined2, joined_out, out_sem.at[0])
     copy.start()
     outs.append(copy)
-    wave(2, 1)
+    wave(0, 2)
     loads[4].wait()
     for i in range(2):
         halos[0][i].wait_recv()
     width = 64 // CHUNKS
     near_field(0, width)
     near_field(width, width)
-    wave(3, 1)
+    wave(3, 2)
     near_field(2 * width, width)
     near_field(3 * width, width)
-    wave(0, 2)
+    wave(2, 2)
     near_field(4 * width, width)
     near_field(5 * width, width)
     wave(1, 2)
     near_field(6 * width, width)
     near_field(7 * width, width)
-    wave(2, 2)
     for copy in x_copies:
         copy.wait_recv()
     for copy in core_copies[1:]:
         copy.start()
-    for i in range(2):
-        halos[2][i].wait_recv()
-    couple(1, x1, place1, 0, 32, 8)
-    wave(3, 2)
     for copy in core_copies:
         copy.wait_recv()
     couple(6, roots, lambda s: s, 0, 1, 1)
@@ -366,18 +392,15 @@
 
         return place
 
+    wave(3, 3)
     wave(2, 3)
-    wave(3, 3)
+    couple(5, g35, place35(5, 12), 0, 2, 2)
+    couple(4, g35, place35(4, 8), 0, 4, 4)
     couple(3, g35, place35(3, 0), 0, 8, 8)
-    couple(4, g35, place35(4, 8), 0, 4, 4)
-    couple(5, g35, place35(5, 12), 0, 2, 2)
-    wave(0, 3)
-    wave(1, 3)
-    couple(2, g2, lambda s: s - grp * SUBS * 16, 0, 16, 8)
 
 
     d[126] = fields[126].astype(BF16)
-    for level in range(LEVELS - 1, 0, -1):
+    for level in range(LEVELS - 1, 1, -1):
         start, _ = span(level)
         parents, count = span(level + 1)
 
@@ -385,17 +408,21 @@
             got = jnp.dot(
                 transfer(start + 2 * p, 2), d[parents + p], preferred_element_type=F32
             )
-            got = got + fields[pl.ds(start + 2 * p, 2)].reshape(128, 128)
-            got = got.reshape(2, 64, 128).astype(BF16)
-            if level == 1:
-                d1_out[pl.ds(2 * p, 2)] = got
+            children = pl.ds(start + 2 * p, 2)
+            if level == 2:
+                fields[children] = got.reshape(2, 64, 128)
             else:
-                d[pl.ds(start + 2 * p, 2)] = got
+                got = got + fields[children].reshape(128, 128)
+                d[children] = got.reshape(2, 64, 128).astype(BF16)
             return carry
 
-        lax.fori_loop(0, count, parent, 0, unroll=min(count, 8))
-
-    for copy in root_copies + [c for pair in halos for c in pair] + x_copies + core_copies:
+        lax.fori_loop(0, count, parent, 0, unroll=count)
+
+    wave(0, 3)
+    wave(1, 3)
+    couple(2, g2, lambda s: s - grp * SUBS * 16, 0, 16, 16)
+
+    for copy in [c for pair in halos for c in pair] + x_copies + core_copies:
         copy.wait_send()
     for tree in copies:
         for copy in tree:
@@ -415,7 +442,7 @@
         out_shape=(
             jax.ShapeDtypeStruct((64, 128, 128), BF16),
             jax.ShapeDtypeStruct((64, 64, 128), BF16),
-            jax.ShapeDtypeStruct((32, 64, 128), BF16),
+            jax.ShapeDtypeStruct((16, 64, 128), BF16),
         ),
         in_specs=[sm, hbm, hbm, hbm, hbm, hbm, sm, sm],
         out_specs=(hbm, hbm, vm),
@@ -429,18 +456,18 @@
             pltpu.VMEM((32 + 2 * REACH, 64, 128), BF16),
             pltpu.VMEM((256, 64, 128), BF16),
             pltpu.VMEM((224, 64, 128), BF16),
-            pltpu.VMEM((128, 64, 128), BF16),
+            pltpu.VMEM((128 * ROOT_ROWS, 16, 128), BF16),
             pltpu.VMEM((6, 64, 64, 127), BF16),
             pltpu.VMEM((3 * C_ROWS, 128), F32),
             pltpu.VMEM((64, 5, 128, 128), BF16),
             pltpu.VMEM((127, 64, 128), F32),
             pltpu.VMEM((64, 128, 128), BF16),
             pltpu.VMEM((64, 64, 128), BF16),
+            pltpu.VMEM((64, 64, 128), BF16),
             pltpu.VMEM((127, 64, 128), BF16),
             dma((5,)), dma((1 + CHUNKS,)),
             dma((6,)), dma((6,)),
             dma((steps,)), dma((steps,)),
-            dma((SUBS - 1,)), dma((SUBS - 1,)),
             dma((XS - 1,)), dma((XS - 1,)),
             dma((XS,)), dma((XS,)),
         ],
@@ -451,33 +478,33 @@
     )(cnt, currents, basis, tr, matrices, near_tiles, far, near)
 
 
-BLOCK = 8
-
-
-def last_kernel(cnt, d1, joined, partial, out):
+BLOCK = 32
+
+
+def last_kernel(cnt, d2, joined, partial, out):
     g = pl.program_id(0)
     lane = lax.broadcasted_iota(jnp.int32, (1, 128), 1)
     for i in range(BLOCK):
-        smooth = lax.dot_general(d1[i // 2], joined[i], TN, preferred_element_type=F32)
+        smooth = lax.dot_general(d2[i // 4], joined[i], TN, preferred_element_type=F32)
         live = (lane < cnt[0, g * BLOCK + i]).astype(F32)
         out[:, i * 128 : (i + 1) * 128] = (smooth + partial[i].astype(F32)) * live
 
 
-def last_pass(cnt, d1, joined, partial):
+def last_pass(cnt, d2, joined, partial):
     return pl.pallas_call(
         last_kernel,
         grid=(64 // BLOCK,),
         out_shape=jax.ShapeDtypeStruct((128, 8192), F32),
         in_specs=[
             pl.BlockSpec(memory_space=pltpu.SMEM),
-            pl.BlockSpec((BLOCK // 2, 64, 128), lambda g: (g, 0, 0)),
+            pl.BlockSpec((BLOCK // 4, 64, 128), lambda g: (g, 0, 0)),
             pl.BlockSpec((BLOCK, 64, 128), lambda g: (g, 0, 0)),
             pl.BlockSpec((BLOCK, 128, 128), lambda g: (g, 0, 0)),
         ],
         out_specs=pl.BlockSpec((128, BLOCK * 128), lambda g: (0, g)),
         compiler_params=pltpu.CompilerParams(vmem_limit_bytes=VMEM_LIMIT),
         name="last_pass",
-    )(cnt, d1, joined, partial)
+    )(cnt, d2, joined, partial)
 
 
 def body(
@@ -495,10 +522,10 @@
     matrices = jnp.transpose(coupling, (1, 2, 3, 0))
     far = jnp.transpose(far_sources, (1, 0))
     near = jnp.transpose(near_sources, (1, 0))
-    partial, joined, d1 = main_pass(
+    partial, joined, d2 = main_pass(
         leaf_segment_count, currents, basis, tr, matrices, near_tiles, far, near
     )
-    return last_pass(leaf_segment_count, d1, joined, partial)
+    return last_pass(leaf_segment_count, d2, joined, partial)
 
 
 def solution(mesh):

time: 74.5 us -> 72.6 us (0.974)
  the two profiles are of different devices: /device:TPU:0 before, /device:TPU:1 now
where the time goes in v1:
time: 72.6 us; the launch traced here: 72.5 us
  Pallas kernels  72.5 us (100%)
    pallas_call x1, Pallas kernels, main_pass(): pl.pallas_call(main_kernel, out_shape=(jax.ShapeDtypeStruct((64, 128, 128...  68.5 us
    pallas_call x1, Pallas kernels, last_pass(): pl.pallas_call(last_kernel, grid=(64 // BLOCK,), out_shape=jax.ShapeDtype...  3.93 us

profile of v1, /device:TPU:1, one launch (start us, length us, event | category | flops | bytes accessed | tf_op | source)
XLA Modules:
  0.0 72.5 jit_solution(17607210869308373333)
XLA Ops:
  0.0 68.5 %main_pass.1 = (bf16[64,128,128]{2,1,0:T(8,128)(2,1)}, bf16[64,64,128]{2,1,0:T(8,128)(2,1)}, bf16[16,64,128]{2,1,0:T(8,128)(2,1)}) custom-call(s32[1,64]{1,0:T(1,128)} %cnt.3, bf16[128,8192]{1,0:T(8,128)(2,1)} %currents.1, bf16[64,64,128]{2,1,0:T(8,128)(2,1)} %bitcast.6, bf16[64,64,126]{2,1,0:T(8,128)(2,1)} %bitcast.7, bf16[6,64,64,127]{3,2,1,0:T(8,128)(2,1)} %bitcast.5, ...), custom_call_target="tpu_custom_call" | custom-call | tf_op jit(solution)/shard_map/main_pass/pallas_call | solution.py:440
  68.5 3.9 %last_pass.1 = f32[128,8192]{1,0:T(8,128)} custom-call(s32[1,64]{1,0:T(1,128)} %cnt.3, bf16[16,64,128]{2,1,0:T(8,128)(2,1)} %get-tuple-element.8.d2, bf16[64,64,128]{2,1,0:T(8,128)(2,1)} %get-tuple-element.9.joined, bf16[64,128,128]{2,1,0:T(8,128)(2,1)} %get-tuple-element.10.partial), custom_call_target="tpu_custom_call" | custom-call | tf_op jit(solution)/shard_map/last_pass/pallas_call | solution.py:494

commit v2 on v1

--- a/solution.py
+++ b/solution.py
@@ -20,7 +20,6 @@
 C_STRIDE = 72
 C_ROWS = 127 * C_STRIDE
 E_STRIDE = 40
-ROOT_ROWS = 4
 NT = (((1,), (1,)), ((), ()))
 TN = (((0,), (0,)), ((), ()))
 
@@ -53,17 +52,35 @@
     (15, 2, 1, 2, 1, -1),
 )
 N_STEPS = len(STEPS)
-WAVES = ((0, 1, 2, 3), (4, 7, 8, 6), (12, 15), (5, 9, 10, 11, 13, 14, 16, 17, 18, 19))
 
 TREES = (
     ("g2", 16, 0, 8, True),
     ("g2", 16, 8, 8, False),
-    ("g35", 14, 0, 8, True),
-    ("g35", 14, 8, 6, False),
-    ("roots", ROOT_ROWS, 0, ROOT_ROWS, True),
+    ("g35", 14, 0, 7, True),
+    ("g35", 14, 7, 7, False),
 )
-ROOT_TREE = 4
 CHUNKS = 8
+
+
+SCHEDULE = (
+    ("r", 0), ("w", 0, 0), ("w", 0, 1), ("w", 0, 2), ("w", 0, 3), ("r", 1), ("w", 1, 0),
+    ("w", 1, 1), ("w", 1, 2), ("w", 1, 3), ("r", 2), ("w", 2, 0), ("w", 2, 1), ("w", 2, 2),
+    ("w", 2, 3), ("r", 3), ("w", 3, 0), ("w", 3, 1), ("w", 3, 2), ("w", 3, 3), ("rz",),
+    ("c0", 0), ("c0", 1), ("w", 0, 4), ("w", 0, 7), ("w", 0, 8), ("w", 0, 6), ("c0", 2),
+    ("c0", 3), ("w", 1, 4), ("w", 1, 7), ("w", 1, 8), ("w", 1, 6), ("c1", 0), ("c1", 1),
+    ("j", 0), ("j", 1), ("w", 2, 4), ("w", 2, 7), ("w", 2, 8), ("w", 2, 6), ("j", 2), ("j", 3),
+    ("n", 0), ("w", 3, 4), ("w", 3, 7), ("w", 3, 8), ("w", 3, 6), ("ry",), ("n", 1), ("n", 2),
+    ("n", 3), ("w", 0, 12), ("w", 0, 15), ("n", 4), ("n", 5), ("w", 1, 12), ("w", 1, 15),
+    ("n", 6), ("n", 7), ("w", 2, 12), ("w", 2, 15), ("rx",), ("w", 3, 12), ("w", 3, 15), ("rf",),
+    ("rc",), ("w", 2, 5), ("w", 2, 9), ("w", 2, 10), ("w", 2, 11), ("w", 2, 13), ("w", 2, 14),
+    ("w", 2, 16), ("w", 2, 17), ("w", 2, 18), ("w", 2, 19), ("w", 3, 5), ("w", 3, 9),
+    ("w", 3, 10), ("w", 3, 11), ("w", 3, 13), ("w", 3, 14), ("w", 3, 16), ("w", 3, 17),
+    ("w", 3, 18), ("w", 3, 19), ("f",), ("w", 0, 5), ("w", 0, 9), ("w", 0, 10), ("w", 0, 11),
+    ("w", 0, 13), ("w", 0, 14), ("w", 0, 16), ("w", 0, 17), ("w", 0, 18), ("w", 0, 19),
+    ("w", 1, 5), ("w", 1, 9), ("w", 1, 10), ("w", 1, 11), ("w", 1, 13), ("w", 1, 14),
+    ("w", 1, 16), ("w", 1, 17), ("w", 1, 18), ("w", 1, 19),
+)
+HALO_OF = {"n": 0, "c0": 1, "c1": 2}
 
 
 def main_kernel(
@@ -71,7 +88,7 @@
     partial_out, joined_out, d2_out,
     cur, bas, tr, e32, xm, x0, x1, g2, g35, roots, cin, c32, tiles, fields, partial, joined, joined2, d,
     in_sem, out_sem, halo_send, halo_recv, tree_send, tree_recv,
-    xs_send, xs_recv, core_send, core_recv,
+    root_send, root_recv,
 ):
     grp = lax.axis_index("grp")
     sub = lax.axis_index("sub")
@@ -131,16 +148,26 @@
             )
         )
 
+    has_above, has_below = sub < SUBS - 1, sub > 0
+
+    def send_halo(which, way):
+        pl.when((has_above, has_below)[way])(halos[which][way].start)
+
+    def halo_sent(which, way):
+        pl.when((has_above, has_below)[way])(halos[which][way].wait_send)
+
+    def halo_arrived(which, way):
+        pl.when((has_below, has_above)[way])(halos[which][way].wait_recv)
+
     def step_copy(tree, i):
         name, n, low, width, z_first = TREES[tree]
-        buffer = {"g2": g2, "g35": g35, "roots": roots}[name]
+        buffer = {"g2": g2, "g35": g35}[name]
         _, first, second, part, dim, way = STEPS[i]
         offset = (second, first) if z_first else (first, second)
         move = (way, 0) if (dim == 1) == z_first else (0, way)
         half = width // 2
         skip, rows = ((0, width), (0, half), (half, width - half))[part]
-        slot = at(*offset) + (grp * SUBS if name == "roots" else 0)
-        block = buffer.at[pl.ds(slot * n + low + skip, rows)]
+        block = buffer.at[pl.ds(at(*offset) * n + low + skip, rows)]
         return remote(block, block, tree_send.at[tree * N_STEPS + i],
                       tree_recv.at[tree * N_STEPS + i], (grp, at(*move)))
 
@@ -150,12 +177,44 @@
         for i in range(4):
             copies[tree][i].start()
 
-    def wave(tree, k):
-        for i in WAVES[k]:
-            copies[tree][i].wait_recv()
-            for j in range(N_STEPS):
-                if STEPS[j][0] == i:
-                    copies[tree][j].start()
+    def arrived(tree, i):
+        copies[tree][i].wait_recv()
+        for j in range(N_STEPS):
+            if STEPS[j][0] == i:
+                copies[tree][j].start()
+
+    def root_block(first, count, pick, device):
+        block = roots.at[pl.ds(first, count)]
+        return remote(block, block, root_send.at[pick], root_recv.at[pick], device)
+
+    def group_block(g, pick, device, first=0, count=SUBS):
+        return root_block(g * SUBS + first, count, pick, device)
+
+    ahead, behind = (along_x(1), sub), (along_x(XS - 1), sub)
+    half_group = SUBS // 2
+    roots_first = [
+        root_block(mine, 1, i - 1, (grp, at((1 - core) * i, core * i))) for i in range(1, SIDE)
+    ]
+    roots_second = [
+        root_block(
+            grp * SUBS + at((j - y) * (1 - core), (j - z) * core), 1, i * SIDE - 1 + j,
+            (grp, at(core * i, (1 - core) * i)),
+        )
+        for i in range(1, SIDE)
+        for j in range(SIDE)
+    ]
+    roots_x = [group_block(grp, 15, ahead), group_block(grp, 16, behind)]
+    roots_far = [
+        group_block(along_x(XS - 1), 17, ahead, 0, half_group),
+        group_block(along_x(1), 18, behind, half_group, half_group),
+    ]
+    roots_core = [group_block(along_x(i), 19 + i, (other_core, sub)) for i in range(XS)]
+
+    def after(waited, started):
+        for copy in waited:
+            copy.wait_recv()
+        for copy in started:
+            copy.start()
 
 
     def relayout_e(k, carry):
@@ -202,24 +261,23 @@
         lax.fori_loop(32 * h, 32 * (h + 1), leaf, 0, unroll=8)
         if h == 0:
             pl.semaphore_wait(barrier, SUBS - 1 + XS - 1 + 1)
-        halos[0][1 - h].start()
-        halos[1][1 - h].start()
+        send_halo(0, 1 - h)
+        send_halo(1, 1 - h)
         lift(1, x0, REACH, x1, REACH, 16 * h, 16, 8)
-        halos[2][1 - h].start()
+        send_halo(2, 1 - h)
         lift(2, x1, REACH, g2, slot2, 8 * h, 8, 8)
-        if h == 0:
-            begin(0)
+        begin(h)
     lift(3, g2, slot2, g35, slot35, 0, 8, 8)
+    begin(2)
     lift(4, g35, slot35, g35, slot35 + 8, 0, 4, 4)
     lift(5, g35, slot35 + 8, g35, slot35 + 12, 0, 2, 2)
+    begin(3)
     start6, _ = span(LEVELS - 1)
     pair = g35[pl.ds(slot35 + 12, 2)].reshape(128, 128)
     root = lax.dot_general(transfer(start6, 2), pair, TN, preferred_element_type=F32)
-    roots[pl.ds(mine * ROOT_ROWS, ROOT_ROWS)] = root.astype(BF16).reshape(ROOT_ROWS, 16, 128)
-    begin(ROOT_TREE)
-    begin(3)
-    begin(2)
-    begin(1)
+    roots[mine] = root.astype(BF16)
+    for copy in roots_first:
+        copy.start()
 
 
     def relayout_c(low, high):
@@ -233,12 +291,10 @@
 
     def couple(level, buffer, place, low, count, unroll):
         start, _ = span(level)
-        rows = ROOT_ROWS if level == LEVELS else 1
-        last = buffer.shape[0] // rows - 1
+        last = buffer.shape[0] - 1
 
         def source(q, t):
-            i = jnp.clip(place(far[q, t]), 0, last)
-            return buffer[i] if rows == 1 else buffer[pl.ds(i * rows, rows)].reshape(64, 128)
+            return buffer[jnp.clip(place(far[q, t]), 0, last)]
 
         def target(i, carry):
             t = start + low + i
@@ -312,77 +368,6 @@
     place0 = lambda s: s - (mine * 64 - REACH)
     place1 = lambda s: s - (mine * 32 - REACH)
 
-    loads[3].wait()
-    relayout_c(0, 16)
-    wave(0, 0)
-    wave(ROOT_TREE, 0)
-    relayout_c(16, 32)
-    wave(3, 0)
-    wave(ROOT_TREE, 1)
-    relayout_c(32, 48)
-    wave(2, 0)
-    wave(ROOT_TREE, 2)
-    relayout_c(48, 64)
-    wave(1, 0)
-    wave(ROOT_TREE, 3)
-
-    def group_roots(g):
-        return roots.at[pl.ds(g * SUBS * ROOT_ROWS, SUBS * ROOT_ROWS)]
-
-    block = group_roots(grp)
-    x_copies = [
-        remote(block, block, xs_send.at[i - 1], xs_recv.at[i - 1], (along_x(i), sub))
-        for i in range(1, XS)
-    ]
-    for copy in x_copies:
-        copy.start()
-    core_copies = [
-        remote(group_roots(along_x(i)), group_roots(along_x(i)), core_send.at[i],
-               core_recv.at[i], (other_core, sub))
-        for i in range(XS)
-    ]
-    core_copies[0].start()
-
-    for i in range(2):
-        halos[1][i].wait_recv()
-    couple(0, x0, place0, 0, 32, 8)
-    wave(0, 1)
-    couple(0, x0, place0, 32, 32, 8)
-    wave(3, 1)
-    for i in range(2):
-        halos[2][i].wait_recv()
-    couple(1, x1, place1, 0, 32, 8)
-    wave(2, 1)
-    join(0, 16)
-    wave(1, 1)
-    join(16, 16)
-    copy = pltpu.make_async_copy(joined2, joined_out, out_sem.at[0])
-    copy.start()
-    outs.append(copy)
-    wave(0, 2)
-    loads[4].wait()
-    for i in range(2):
-        halos[0][i].wait_recv()
-    width = 64 // CHUNKS
-    near_field(0, width)
-    near_field(width, width)
-    wave(3, 2)
-    near_field(2 * width, width)
-    near_field(3 * width, width)
-    wave(2, 2)
-    near_field(4 * width, width)
-    near_field(5 * width, width)
-    wave(1, 2)
-    near_field(6 * width, width)
-    near_field(7 * width, width)
-    for copy in x_copies:
-        copy.wait_recv()
-    for copy in core_copies[1:]:
-        copy.start()
-    for copy in core_copies:
-        copy.wait_recv()
-    couple(6, roots, lambda s: s, 0, 1, 1)
-
     def place35(level, offset):
         _, count = span(level)
 
@@ -392,41 +377,83 @@
 
         return place
 
-    wave(3, 3)
-    wave(2, 3)
-    couple(5, g35, place35(5, 12), 0, 2, 2)
-    couple(4, g35, place35(4, 8), 0, 4, 4)
-    couple(3, g35, place35(3, 0), 0, 8, 8)
-
-
-    d[126] = fields[126].astype(BF16)
-    for level in range(LEVELS - 1, 1, -1):
-        start, _ = span(level)
-        parents, count = span(level + 1)
-
-        def parent(p, carry, start=start, parents=parents, level=level):
-            got = jnp.dot(
-                transfer(start + 2 * p, 2), d[parents + p], preferred_element_type=F32
-            )
-            children = pl.ds(start + 2 * p, 2)
-            if level == 2:
-                fields[children] = got.reshape(2, 64, 128)
-            else:
-                got = got + fields[children].reshape(128, 128)
-                d[children] = got.reshape(2, 64, 128).astype(BF16)
-            return carry
-
-        lax.fori_loop(0, count, parent, 0, unroll=count)
-
-    wave(0, 3)
-    wave(1, 3)
+    def coarse_fields():
+        couple(6, roots, lambda s: s, 0, 1, 1)
+        couple(5, g35, place35(5, 12), 0, 2, 2)
+        couple(4, g35, place35(4, 8), 0, 4, 4)
+        couple(3, g35, place35(3, 0), 0, 8, 8)
+        d[126] = fields[126].astype(BF16)
+        for level in range(LEVELS - 1, 1, -1):
+            start, _ = span(level)
+            parents, count = span(level + 1)
+
+            def parent(p, carry, start=start, parents=parents, level=level):
+                got = jnp.dot(
+                    transfer(start + 2 * p, 2), d[parents + p], preferred_element_type=F32
+                )
+                children = pl.ds(start + 2 * p, 2)
+                if level == 2:
+                    fields[children] = got.reshape(2, 64, 128)
+                else:
+                    got = got + fields[children].reshape(128, 128)
+                    d[children] = got.reshape(2, 64, 128).astype(BF16)
+                return carry
+
+            lax.fori_loop(0, count, parent, 0, unroll=count)
+
+    def beside(kind, i):
+        if i == 0:
+            if kind == "r":
+                loads[3].wait()
+            if kind == "n":
+                loads[4].wait()
+            if kind in HALO_OF:
+                for way in range(2):
+                    halo_arrived(HALO_OF[kind], way)
+        if kind == "r":
+            relayout_c(16 * i, 16 * (i + 1))
+        elif kind == "c0":
+            couple(0, x0, place0, 16 * i, 16, 8)
+        elif kind == "c1":
+            couple(1, x1, place1, 16 * i, 16, 8)
+        elif kind == "j":
+            join(8 * i, 8)
+            if i == 3:
+                copy = pltpu.make_async_copy(joined2, joined_out, out_sem.at[0])
+                copy.start()
+                outs.append(copy)
+        else:
+            near_field(8 * i, 8)
+
+    for op in SCHEDULE:
+        kind = op[0]
+        if kind == "w":
+            arrived(op[1], op[2])
+        elif kind == "rz":
+            after(roots_first, roots_second)
+        elif kind == "ry":
+            after(roots_second, roots_x + roots_core[:1])
+        elif kind == "rx":
+            after(roots_x, roots_far + roots_core[1::2])
+        elif kind == "rf":
+            after(roots_far, roots_core[2:3])
+        elif kind == "rc":
+            after(roots_core, [])
+        elif kind == "f":
+            coarse_fields()
+        else:
+            beside(kind, op[1])
+
     couple(2, g2, lambda s: s - grp * SUBS * 16, 0, 16, 16)
 
-    for copy in [c for pair in halos for c in pair] + x_copies + core_copies:
-        copy.wait_send()
+    for which in range(len(halos)):
+        for way in range(2):
+            halo_sent(which, way)
     for tree in copies:
         for copy in tree:
             copy.wait_send()
+    for copy in roots_first + roots_second + roots_x + roots_far + roots_core:
+        copy.wait_send()
     for copy in outs:
         copy.wait()
 
@@ -456,7 +483,7 @@
             pltpu.VMEM((32 + 2 * REACH, 64, 128), BF16),
             pltpu.VMEM((256, 64, 128), BF16),
             pltpu.VMEM((224, 64, 128), BF16),
-            pltpu.VMEM((128 * ROOT_ROWS, 16, 128), BF16),
+            pltpu.VMEM((128, 64, 128), BF16),
             pltpu.VMEM((6, 64, 64, 127), BF16),
             pltpu.VMEM((3 * C_ROWS, 128), F32),
             pltpu.VMEM((64, 5, 128, 128), BF16),
@@ -468,8 +495,7 @@
             dma((5,)), dma((1 + CHUNKS,)),
             dma((6,)), dma((6,)),
             dma((steps,)), dma((steps,)),
-            dma((XS - 1,)), dma((XS - 1,)),
-            dma((XS,)), dma((XS,)),
+            dma((19 + XS,)), dma((19 + XS,)),
         ],
         compiler_params=pltpu.CompilerParams(
             collective_id=0, has_side_effects=True, vmem_limit_bytes=VMEM_LIMIT

time: 72.6 us -> 70.6 us (0.972)
  Pallas kernels: 72.5 us -> 70.4 us
    pallas_call x1, Pallas kernels: 68.5 us -> 66.5 us  [main_pass(): pl.pallas_call(main_kernel, out_shape=(jax.ShapeDtypeStruct((64, 128, 128...]
where the time goes in v2:
time: 70.6 us; the launch traced here: 70.4 us
  Pallas kernels  70.4 us (100%)
    pallas_call x1, Pallas kernels, main_pass(): pl.pallas_call(main_kernel, out_shape=(jax.ShapeDtypeStruct((64, 128, 128...  66.5 us
    pallas_call x1, Pallas kernels, last_pass(): pl.pallas_call(last_kernel, grid=(64 // BLOCK,), out_shape=jax.ShapeDtype...  3.94 us

profile of v2, /device:TPU:1, one launch (start us, length us, event | category | flops | bytes accessed | tf_op | source)
XLA Modules:
  0.0 70.4 jit_solution(16239303078721968518)
XLA Ops:
  0.0 66.5 %main_pass.1 = (bf16[64,128,128]{2,1,0:T(8,128)(2,1)}, bf16[64,64,128]{2,1,0:T(8,128)(2,1)}, bf16[16,64,128]{2,1,0:T(8,128)(2,1)}) custom-call(s32[1,64]{1,0:T(1,128)} %cnt.3, bf16[128,8192]{1,0:T(8,128)(2,1)} %currents.1, bf16[64,64,128]{2,1,0:T(8,128)(2,1)} %bitcast.6, bf16[64,64,126]{2,1,0:T(8,128)(2,1)} %bitcast.7, bf16[6,64,64,127]{3,2,1,0:T(8,128)(2,1)} %bitcast.5, ...), custom_call_target="tpu_custom_call" | custom-call | tf_op jit(solution)/shard_map/main_pass/pallas_call | solution.py:467
  66.5 3.9 %last_pass.1 = f32[128,8192]{1,0:T(8,128)} custom-call(s32[1,64]{1,0:T(1,128)} %cnt.3, bf16[16,64,128]{2,1,0:T(8,128)(2,1)} %get-tuple-element.8.d2, bf16[64,64,128]{2,1,0:T(8,128)(2,1)} %get-tuple-element.9.joined, bf16[64,128,128]{2,1,0:T(8,128)(2,1)} %get-tuple-element.10.partial), custom_call_target="tpu_custom_call" | custom-call | tf_op jit(solution)/shard_map/last_pass/pallas_call | solution.py:520

commit v3 on v2

--- a/solution.py
+++ b/solution.py
@@ -65,14 +65,14 @@
 SCHEDULE = (
     ("r", 0), ("w", 0, 0), ("w", 0, 1), ("w", 0, 2), ("w", 0, 3), ("r", 1), ("w", 1, 0),
     ("w", 1, 1), ("w", 1, 2), ("w", 1, 3), ("r", 2), ("w", 2, 0), ("w", 2, 1), ("w", 2, 2),
-    ("w", 2, 3), ("r", 3), ("w", 3, 0), ("w", 3, 1), ("w", 3, 2), ("w", 3, 3), ("rz",),
-    ("c0", 0), ("c0", 1), ("w", 0, 4), ("w", 0, 7), ("w", 0, 8), ("w", 0, 6), ("c0", 2),
-    ("c0", 3), ("w", 1, 4), ("w", 1, 7), ("w", 1, 8), ("w", 1, 6), ("c1", 0), ("c1", 1),
-    ("j", 0), ("j", 1), ("w", 2, 4), ("w", 2, 7), ("w", 2, 8), ("w", 2, 6), ("j", 2), ("j", 3),
-    ("n", 0), ("w", 3, 4), ("w", 3, 7), ("w", 3, 8), ("w", 3, 6), ("ry",), ("n", 1), ("n", 2),
-    ("n", 3), ("w", 0, 12), ("w", 0, 15), ("n", 4), ("n", 5), ("w", 1, 12), ("w", 1, 15),
-    ("n", 6), ("n", 7), ("w", 2, 12), ("w", 2, 15), ("rx",), ("w", 3, 12), ("w", 3, 15), ("rf",),
-    ("rc",), ("w", 2, 5), ("w", 2, 9), ("w", 2, 10), ("w", 2, 11), ("w", 2, 13), ("w", 2, 14),
+    ("w", 2, 3), ("r", 3), ("w", 3, 0), ("w", 3, 1), ("w", 3, 2), ("w", 3, 3), ("rz",), ("j", 0),
+    ("j", 1), ("w", 0, 4), ("w", 0, 7), ("w", 0, 8), ("w", 0, 6), ("j", 2), ("j", 3), ("c0", 0),
+    ("c0", 1), ("w", 1, 4), ("w", 1, 7), ("w", 1, 8), ("w", 1, 6), ("c0", 2), ("c0", 3),
+    ("w", 2, 4), ("w", 2, 7), ("w", 2, 8), ("w", 2, 6), ("c1", 0), ("c1", 1), ("n", 0),
+    ("w", 3, 4), ("w", 3, 7), ("w", 3, 8), ("w", 3, 6), ("ry",), ("n", 1), ("n", 2), ("n", 3),
+    ("w", 0, 12), ("w", 0, 15), ("n", 4), ("n", 5), ("w", 1, 12), ("w", 1, 15), ("n", 6),
+    ("n", 7), ("w", 2, 12), ("w", 2, 15), ("rx",), ("w", 3, 12), ("w", 3, 15), ("rf",), ("rc",),
+    ("w", 2, 5), ("w", 2, 9), ("w", 2, 10), ("w", 2, 11), ("w", 2, 13), ("w", 2, 14),
     ("w", 2, 16), ("w", 2, 17), ("w", 2, 18), ("w", 2, 19), ("w", 3, 5), ("w", 3, 9),
     ("w", 3, 10), ("w", 3, 11), ("w", 3, 13), ("w", 3, 14), ("w", 3, 16), ("w", 3, 17),
     ("w", 3, 18), ("w", 3, 19), ("f",), ("w", 0, 5), ("w", 0, 9), ("w", 0, 10), ("w", 0, 11),
@@ -262,9 +262,7 @@
         if h == 0:
             pl.semaphore_wait(barrier, SUBS - 1 + XS - 1 + 1)
         send_halo(0, 1 - h)
-        send_halo(1, 1 - h)
         lift(1, x0, REACH, x1, REACH, 16 * h, 16, 8)
-        send_halo(2, 1 - h)
         lift(2, x1, REACH, g2, slot2, 8 * h, 8, 8)
         begin(h)
     lift(3, g2, slot2, g35, slot35, 0, 8, 8)
@@ -278,6 +276,9 @@
     roots[mine] = root.astype(BF16)
     for copy in roots_first:
         copy.start()
+    for which in (1, 2):
+        for way in range(2):
+            send_halo(which, way)
 
 
     def relayout_c(low, high):

time: 70.6 us -> 70.5 us (level)
  no operation moved by 1% of the time
where the time goes in v3:
time: 70.5 us; the launch traced here: 70.4 us
  Pallas kernels  70.4 us (100%)
    pallas_call x1, Pallas kernels, main_pass(): pl.pallas_call(main_kernel, out_shape=(jax.ShapeDtypeStruct((64, 128, 128...  66.4 us
    pallas_call x1, Pallas kernels, last_pass(): pl.pallas_call(last_kernel, grid=(64 // BLOCK,), out_shape=jax.ShapeDtype...  3.94 us

profile of v3, /device:TPU:1, one launch (start us, length us, event | category | flops | bytes accessed | tf_op | source)
XLA Modules:
  0.0 70.4 jit_solution(2406741970695298867)
XLA Ops:
  0.0 66.4 %main_pass.1 = (bf16[64,128,128]{2,1,0:T(8,128)(2,1)}, bf16[64,64,128]{2,1,0:T(8,128)(2,1)}, bf16[16,64,128]{2,1,0:T(8,128)(2,1)}) custom-call(s32[1,64]{1,0:T(1,128)} %cnt.3, bf16[128,8192]{1,0:T(8,128)(2,1)} %currents.1, bf16[64,64,128]{2,1,0:T(8,128)(2,1)} %bitcast.6, bf16[64,64,126]{2,1,0:T(8,128)(2,1)} %bitcast.7, bf16[6,64,64,127]{3,2,1,0:T(8,128)(2,1)} %bitcast.5, ...), custom_call_target="tpu_custom_call" | custom-call | tf_op jit(solution)/shard_map/main_pass/pallas_call | solution.py:468
  66.4 3.9 %last_pass.1 = f32[128,8192]{1,0:T(8,128)} custom-call(s32[1,64]{1,0:T(1,128)} %cnt.3, bf16[16,64,128]{2,1,0:T(8,128)(2,1)} %get-tuple-element.8.d2, bf16[64,64,128]{2,1,0:T(8,128)(2,1)} %get-tuple-element.9.joined, bf16[64,128,128]{2,1,0:T(8,128)(2,1)} %get-tuple-element.10.partial), custom_call_target="tpu_custom_call" | custom-call | tf_op jit(solution)/shard_map/last_pass/pallas_call | solution.py:521
